TPU v7x, 512 devices: a whole 4x8x8 slice. The times are simulated.
512 devices in a mesh: mp: 32 (over z, y_lo), dp: 16 (over x, y_hi, core).
Axes of the slice: x: 4, y: 8 (y_hi: 2, y_lo: 4; y = y_hi * 4 + y_lo), z: 8, core: 2. Of those that a mesh axis runs over, the one named last changes fastest.
Arguments:
- forward_fields: bfloat16 [16, 4, 65536], P(None, None, 'mp'), may hold values from -6 to 6
- adjoint_fields: bfloat16 [64, 4, 65536], P(None, None, 'mp'), may hold values from -6 to 6
- data_rec: int32 [3072], P('dp'), may hold values from 0 to 63
- data_freq: int32 [3072], P('dp'), may hold values from 0 to 15
- data_coef: float32 [3072, 4], P('dp'), may hold values from -6 to 6
- residual_cols: bfloat16 [3072, 256], P('dp'), may hold values from -6 to 6
Outputs:
- data_update: bfloat16 [3072, 256], P('dp')
- model_update: float32 [65536, 256], P(('mp', 'dp'))
All inputs are finite; a program needn't handle non-finite values.
Results may differ from a plain program's by a relative error of at most 0.0075.
Values may be sent and summed in bfloat16 or wider, within the bound.
No kernel may reach another device: no remote copies, remote signals or barrier semaphores. Data moves between devices by JAX's collectives and lax.ppermute only.
A program may use at most 64 MiB of HBM per device.

v0:
```python
import math
import jax
import jax.numpy as jnp
from jax import lax
from jax.sharding import PartitionSpec as P

GRID_COLS = 128
SWEEPS = 2


def with_halo(array, sides, width):
    for axis, dim in sides:
        peers, length = (lax.axis_size(axis), array.shape[dim])
        up = [(i, (i + 1) % peers) for i in range(peers - 1)]
        down = [(j, i) for i, j in up]
        last = lax.slice_in_dim(array, length - width, length, axis=dim)
        leading = lax.slice_in_dim(array, 0, width, axis=dim)
        before = lax.ppermute(last, axis, up)
        after = lax.ppermute(leading, axis, down)
        array = jnp.concatenate([before, array, after], axis=dim)
    return array


def sweep_once(field):
    center = field[:, 1:-1, :]
    sides = jnp.pad(center, ((0, 0), (0, 0), (1, 1)))
    beside_all = field[:, :-2, :] + field[:, 2:, :] + sides[:, :, :-2] + sides[:, :, 2:]
    return center + 0.2 * (beside_all - 4.0 * center)


def per_device(forward_fields, adjoint_fields, data_rec, data_freq, data_coef, residual_cols):
    rows_here = data_rec.shape[0]
    cells_here = forward_fields.shape[2]
    slab_rows = cells_here // GRID_COLS
    slab_count = lax.axis_size("mp")
    block_count = lax.axis_size("dp")
    adjoint = adjoint_fields[data_rec].astype(jnp.float32)
    forward = forward_fields[data_freq].astype(jnp.float32)
    sens = (0.5 * jnp.sum(data_coef[:, :, None] * adjoint * forward, axis=1)).astype(jnp.bfloat16)
    grid = sens.astype(jnp.float32).reshape(rows_here, slab_rows, GRID_COLS)
    for sweep in range(SWEEPS):
        padded = with_halo(grid, (("mp", 1),), 1)
        grid = sweep_once(padded)
    smooth = grid.reshape(rows_here, cells_here).astype(jnp.bfloat16)
    residual_whole = lax.all_gather(residual_cols, "dp", axis=0, tiled=True)
    gram_tile = lax.dot_general(
        smooth,
        lax.all_gather(sens, "dp", axis=0, tiled=True),
        (((1,), (1,)), ((), ())),
        preferred_element_type=jnp.float32,
    )
    partial_value = jnp.dot(
        gram_tile, residual_whole.astype(jnp.float32), precision=lax.Precision.HIGHEST
    )
    gram_prod = lax.psum(partial_value, "mp") / (cells_here * slab_count)
    data_update = (gram_prod + residual_cols.astype(jnp.float32)).astype(jnp.bfloat16)
    summed = lax.psum_scatter(
        lax.dot_general(
            smooth, data_update, (((0,), (0,)), ((), ())), preferred_element_type=jnp.float32
        ),
        "dp",
        scatter_dimension=0,
        tiled=True,
    )
    model_update = summed / math.sqrt(rows_here * block_count)
    return (data_update, model_update)


def solution(mesh):
    in_specs = (
        P(None, None, "mp"),
        P(None, None, "mp"),
        P("dp"),
        P("dp"),
        P("dp", None),
        P("dp", None),
    )
    out_specs = (P("dp", None), P(("mp", "dp"), None))
    return jax.shard_map(
        per_device, mesh=mesh, in_specs=in_specs, out_specs=out_specs, check_vma=False
    )
```

profile of v0, /device:TPU:1, one launch (start us, length us, event | category | flops | bytes accessed | tf_op | source)
XLA Modules:
  0.0 661.7 jit_solution(15564410182115889151)
XLA Ops:
  7.2 0.8 compare_select_fusion.1
  8.0 0.7 compare_select_fusion
  8.7 0.8 copy.8
  9.5 9.6 %gather_fusion = bf16[192,4,2048]{2,1,0:T(4,128)(2,1)} fusion(bf16[64,4,2048]{2,1,0:T(4,128)(2,1)S(1)} %copy-done, s32[1024]{0:T(1024)S(1)} %pad_clamp_fusion.1), kind=kCustom, calls=%fused_computation | custom fusion | bytes 6292224 | tf_op jit(solution)/shard_map/gather | solution.py:37
  19.1 9.7 %gather_fusion.1 = bf16[192,4,2048]{2,1,0:T(4,128)(2,1)} fusion(bf16[16,4,2048]{2,1,0:T(4,128)(2,1)S(1)} %copy-done.1, s32[1024]{0:T(1024)S(1)} %pad_clamp_fusion), kind=kCustom, calls=%fused_computation.1 | custom fusion | bytes 6292224 | tf_op jit(solution)/shard_map/gather | solution.py:38
  28.8 9.7 %multiply_reduce_fusion = f32[192,2048]{1,0:T(8,128)S(1)} fusion(bf16[192,4,2048]{2,1,0:T(4,128)(2,1)} %gather_fusion.1, bf16[192,4,2048]{2,1,0:T(4,128)(2,1)} %gather_fusion, f32[192,4]{1,0:T(8,128)S(1)} %copy.8), kind=kLoop, calls=%fused_computation.2 | loop fusion | flops 7471104 | bytes 7867392 | tf_op jit(solution)/shard_map/reduce_sum | solution.py:39
  38.5 1.2 convert_bitcast_fusion
  39.7 0.0 all-gather.5.cloned.1.call-start
  39.8 0.7 all-gather.5.cloned.1.call-update
  40.5 0.3 copy.9
  40.8 0.1 fusion.20
  40.9 4.0 collective-permute-start
  45.0 1.3 collective-permute-start.1
  46.3 0.3 collective-permute-done
  46.6 5.8 collective-permute-done.1
  52.5 1.3 fusion.4
  53.8 0.1 fusion.19
  53.9 3.8 collective-permute-start.2
  57.7 1.5 collective-permute-start.3
  59.2 0.1 collective-permute-done.2
  59.3 7.2 %collective-permute-done.3 = f32[192,1,128]{2,1,0:T(1,128)S(1)} collective-permute-done((f32[192,1,128]{2,1,0:T(1,128)S(1)}, f32[192,1,128]{2,1,0:T(1,128)S(1)}, u32[]{:S(2)}, u32[]{:S(2)}) %collective-permute-start.3) | collective-permute-done | bytes 98336 | tf_op jit(solution)/shard_map/ppermute | solution.py:19
  66.5 1.3 fusion.10
  67.8 128.4 %all-gather.3.cloned.1.call-done = bf16[3072,2048]{1,0:T(8,128)(2,1)} async-done(((bf16[192,2048]{1,0:T(8,128)(2,1)}), bf16[3072,2048]{1,0:T(8,128)(2,1)}) %all-gather.3.cloned.1.call-update) | async-done | bytes 12582928 | tf_op jit(solution)/shard_map/all_gather | solution.py:48
  196.3 10.3 %fusion.15 = f32[192,3072]{1,0:T(8,128)} fusion(bf16[3072,2048]{1,0:T(8,128)(2,1)} %all-gather.3.cloned.1.call-done, bf16[24,8,16,128]{3,2,1,0:T(8,128)(2,1)S(1)} %bitcast.15), kind=kOutput, calls=%fused_computation.28 | convolution fusion | flops 2415919104 | bytes 15728640 | tf_op jit(solution)/shard_map/dot_general | solution.py:46
  206.5 50.8 %all-gather.5.cloned.1.call-done = bf16[3072,256]{1,0:T(8,128)(2,1)} async-done(((bf16[192,256]{1,0:T(8,128)(2,1)}), bf16[3072,256]{1,0:T(8,128)(2,1)}) %all-gather.5.cloned.1.call-update) | async-done | bytes 1572880 | tf_op jit(solution)/shard_map/all_gather | solution.py:45
  257.3 4.0 fusion.21
  261.4 0.0 reduce-scatter.2.cloned.1.call-start
  261.4 272.9 %all-reduce.4.cloned.1.call-done = f32[192,256]{1,0:T(8,128)} async-done(((f32[192,256]{1,0:T(8,128)}), f32[192,256]{1,0:T(8,128)}) %all-reduce.4.cloned.1.call-update) | async-done | bytes 196624 | tf_op jit(solution)/shard_map/psum | solution.py:55
  534.3 1.0 add_convert_fusion
  535.2 1.8 fusion.13
  537.1 116.5 %reduce-scatter.2.cloned.1.call-done = f32[128,256]{1,0:T(8,128)} async-done(((f32[2048,256]{1,0:T(8,128)}), f32[128,256]{1,0:T(8,128)}) %reduce-scatter.2.cloned.1.call-update) | async-done | bytes 131088 | tf_op jit(solution)/shard_map/reduce_scatter | solution.py:57
  653.6 1.6 broadcast_multiply_fusion
  (15 shorter events, 0.2 us)
Async XLA Ops:
  7.2 2.3 copy-start
  7.2 189.1 %all-gather.3.cloned.1.call-start = ((), (), s32[]{:S(2)}) async-start(), calls=%async_computation.1 | async-start | bytes 13369344 | tf_op jit(solution)/shard_map/all_gather | solution.py:48
  9.5 9.6 %copy-start.1 = (bf16[16,4,2048]{2,1,0:T(4,128)(2,1)S(1)}, bf16[16,4,2048]{2,1,0:T(4,128)(2,1)}, u32[]{:S(2)}) copy-start(bf16[16,4,2048]{2,1,0:T(4,128)(2,1)} %param.6) | copy-start | bytes 786436
  39.7 217.6 %all-gather.5.cloned.1.call-start = ((), (), s32[]{:S(2)}) async-start(), calls=%async_computation.2 | async-start | bytes 1671168 | tf_op jit(solution)/shard_map/all_gather | solution.py:45
  40.5 493.8 %all-reduce.4.cloned.1.call-start = ((), (), s32[]{:S(2)}) async-start(), calls=%async_computation.3 | async-start | bytes 393216 | tf_op jit(solution)/shard_map/psum | solution.py:55
  40.9 5.7 collective-permute-start
  45.0 7.5 %collective-permute-start.1 = (f32[192,1,128]{2,1,0:T(1,128)S(1)}, f32[192,1,128]{2,1,0:T(1,128)S(1)}, u32[]{:S(2)}, u32[]{:S(2)}) collective-permute-start(f32[192,1,128]{2,1,0:T(1,128)S(1)} %get-tuple-element.7), channel_id=1, source_target_pairs={{16,0},{32,16},{48,32},{64,48},{80,64},{96,80},{112,96},{128,112},... | collective-permute-start | bytes 294920 | tf_op jit(solution)/shard_map/ppermute | solution.py:19
  53.9 5.4 collective-permute-start.2
  57.7 8.8 %collective-permute-start.3 = (f32[192,1,128]{2,1,0:T(1,128)S(1)}, f32[192,1,128]{2,1,0:T(1,128)S(1)}, u32[]{:S(2)}, u32[]{:S(2)}) collective-permute-start(f32[192,1,128]{2,1,0:T(1,128)S(1)} %get-tuple-element.5), channel_id=1, source_target_pairs={{16,0},{32,16},{48,32},{64,48},{80,64},{96,80},{112,96},{128,112},... | collective-permute-start | bytes 294920 | tf_op jit(solution)/shard_map/ppermute | solution.py:19
  206.5 327.7 %copy-start.3 = (bf16[192,256]{1,0:T(8,128)(2,1)S(1)}, bf16[192,256]{1,0:T(8,128)(2,1)}, u32[]{:S(2)}) copy-start(bf16[192,256]{1,0:T(8,128)(2,1)} %param.11) | copy-start | bytes 294916
  261.4 392.2 %reduce-scatter.2.cloned.1.call-start = ((), (), s32[]{:S(2)}) async-start(), calls=%async_computation.4 | async-start | bytes 2228224 | tf_op jit(solution)/shard_map/reduce_scatter | solution.py:57
  535.2 1.9 copy-start.2
Sparse Core Ops, SparseCore 0:
  39.8 156.4 all-gather.2
  199.5 57.7 all-gather.4
  261.5 272.7 all-reduce.3
  539.7 113.8 reduce-scatter.1
where the time goes:
time: 662 us
  waiting for transfers between devices  583 us (88%)
  local copies, waits for them, and re-layouts  20.7 us (3%)
  other arithmetic  17.5 us (3%)
  matrix products  16.1 us (2%)
  between operations  13.9 us (2%)
  starting transfers between devices  10.8 us (2%)
    psum x1, waiting for transfers between devices, per_device(): gram_prod = lax.psum(partial_value, 'mp') / (cells_here * slab_count)  273 us
    all_gather x1, waiting for transfers between devices, per_device(): lax.all_gather(sens, 'dp', axis=0, tiled=True)  128 us
    reduce_scatter x1, waiting for transfers between devices, per_device(): lax.psum_scatter(lax.dot_general(smooth, data_update, (((0,), (0,)), ((),...  116 us
    all_gather x1, waiting for transfers between devices, per_device(): residual_whole = lax.all_gather(residual_cols, 'dp', axis=0, tiled=True)  50.8 us
  transfers between devices with their start and end apart: 8, of which 8 were waited for; matrix products, arithmetic and copies ran while one was open for 2% of the time, Pallas kernels for 0%

commit v1 on v0

--- a/solution.py
+++ b/solution.py
@@ -52,7 +52,7 @@
     partial_value = jnp.dot(
         gram_tile, residual_whole.astype(jnp.float32), precision=lax.Precision.HIGHEST
     )
-    gram_prod = lax.psum(partial_value, "mp") / (cells_here * slab_count)
+    gram_prod = jnp.sum(lax.all_gather(partial_value, "mp"), axis=0) / (cells_here * slab_count)
     data_update = (gram_prod + residual_cols.astype(jnp.float32)).astype(jnp.bfloat16)
     summed = lax.psum_scatter(
         lax.dot_general(

time: 662 us -> 542 us (0.82)
  waiting for transfers between devices: 583 us -> 460 us
    psum x1 -> x0, waiting for transfers between devices: 273 us -> none  [per_device(): gram_prod = lax.psum(partial_value, 'mp') / (cells_here * slab_count)]
    all_gather x0 -> x1, waiting for transfers between devices: none -> 155 us  [per_device(): lax.all_gather(partial_value, 'mp')]
where the time goes in v1:
time: 542 us
  waiting for transfers between devices  460 us (85%)
  local copies, waits for them, and re-layouts  20.7 us (4%)
  other arithmetic  19.8 us (4%)
  matrix products  16.1 us (3%)
  between operations  13.9 us (3%)
  starting transfers between devices  10.8 us (2%)
    all_gather x1, waiting for transfers between devices, per_device(): lax.all_gather(partial_value, 'mp')  155 us
    all_gather x1, waiting for transfers between devices, per_device(): lax.all_gather(sens, 'dp', axis=0, tiled=True)  128 us
    reduce_scatter x1, waiting for transfers between devices, per_device(): lax.psum_scatter(lax.dot_general(smooth, data_update, (((0,), (0,)), ((),...  112 us
    all_gather x1, waiting for transfers between devices, per_device(): residual_whole = lax.all_gather(residual_cols, 'dp', axis=0, tiled=True)  50.8 us
    ppermute x2, waiting for transfers between devices, with_halo(): after = lax.ppermute(leading, axis, down)  13 us
  transfers between devices with their start and end apart: 8, of which 8 were waited for; matrix products, arithmetic and copies ran while one was open for 2% of the time, Pallas kernels for 0%

profile of v1, /device:TPU:1, one launch (start us, length us, event | category | flops | bytes accessed | tf_op | source)
XLA Modules:
  0.0 541.6 jit_solution(9970706835066252545)
XLA Ops:
  7.2 0.8 compare_select_fusion.1
  8.0 0.7 compare_select_fusion
  8.7 0.8 copy.8
  9.5 9.6 %gather_fusion = bf16[192,4,2048]{2,1,0:T(4,128)(2,1)} fusion(bf16[64,4,2048]{2,1,0:T(4,128)(2,1)S(1)} %copy-done, s32[1024]{0:T(1024)S(1)} %pad_clamp_fusion.1), kind=kCustom, calls=%fused_computation | custom fusion | bytes 6292224 | tf_op jit(solution)/shard_map/gather | solution.py:37
  19.1 9.7 %gather_fusion.1 = bf16[192,4,2048]{2,1,0:T(4,128)(2,1)} fusion(bf16[16,4,2048]{2,1,0:T(4,128)(2,1)S(1)} %copy-done.1, s32[1024]{0:T(1024)S(1)} %pad_clamp_fusion), kind=kCustom, calls=%fused_computation.1 | custom fusion | bytes 6292224 | tf_op jit(solution)/shard_map/gather | solution.py:38
  28.8 9.7 %multiply_reduce_fusion = f32[192,2048]{1,0:T(8,128)S(1)} fusion(bf16[192,4,2048]{2,1,0:T(4,128)(2,1)} %gather_fusion.1, bf16[192,4,2048]{2,1,0:T(4,128)(2,1)} %gather_fusion, f32[192,4]{1,0:T(8,128)S(1)} %copy.8), kind=kLoop, calls=%fused_computation.2 | loop fusion | flops 7471104 | bytes 7867392 | tf_op jit(solution)/shard_map/reduce_sum | solution.py:39
  38.5 1.2 convert_bitcast_fusion
  39.7 0.0 all-gather.7.cloned.1.call-start
  39.8 0.7 all-gather.7.cloned.1.call-update
  40.5 0.3 copy.9
  40.8 0.1 fusion.20
  40.9 4.0 collective-permute-start
  45.0 1.3 collective-permute-start.1
  46.3 0.3 collective-permute-done
  46.6 5.8 %collective-permute-done.1 = f32[192,1,128]{2,1,0:T(1,128)S(1)} collective-permute-done((f32[192,1,128]{2,1,0:T(1,128)S(1)}, f32[192,1,128]{2,1,0:T(1,128)S(1)}, u32[]{:S(2)}, u32[]{:S(2)}) %collective-permute-start.1) | collective-permute-done | bytes 98336 | tf_op jit(solution)/shard_map/ppermute | solution.py:19
  52.5 1.3 fusion.4
  53.8 0.1 fusion.19
  53.9 3.8 collective-permute-start.2
  57.7 1.5 collective-permute-start.3
  59.2 0.1 collective-permute-done.2
  59.3 7.2 %collective-permute-done.3 = f32[192,1,128]{2,1,0:T(1,128)S(1)} collective-permute-done((f32[192,1,128]{2,1,0:T(1,128)S(1)}, f32[192,1,128]{2,1,0:T(1,128)S(1)}, u32[]{:S(2)}, u32[]{:S(2)}) %collective-permute-start.3) | collective-permute-done | bytes 98336 | tf_op jit(solution)/shard_map/ppermute | solution.py:19
  66.5 1.3 fusion.10
  67.8 128.4 %all-gather.5.cloned.1.call-done = bf16[3072,2048]{1,0:T(8,128)(2,1)} async-done(((bf16[192,2048]{1,0:T(8,128)(2,1)}), bf16[3072,2048]{1,0:T(8,128)(2,1)}) %all-gather.5.cloned.1.call-update) | async-done | bytes 12582928 | tf_op jit(solution)/shard_map/all_gather | solution.py:48
  196.3 10.3 %fusion.15 = f32[192,3072]{1,0:T(8,128)} fusion(bf16[3072,2048]{1,0:T(8,128)(2,1)} %all-gather.5.cloned.1.call-done, bf16[24,8,16,128]{3,2,1,0:T(8,128)(2,1)S(1)} %bitcast.17), kind=kOutput, calls=%fused_computation.28 | convolution fusion | flops 2415919104 | bytes 15728640 | tf_op jit(solution)/shard_map/dot_general | solution.py:46
  206.5 50.8 %all-gather.7.cloned.1.call-done = bf16[3072,256]{1,0:T(8,128)(2,1)} async-done(((bf16[192,256]{1,0:T(8,128)(2,1)}), bf16[3072,256]{1,0:T(8,128)(2,1)}) %all-gather.7.cloned.1.call-update) | async-done | bytes 1572880 | tf_op jit(solution)/shard_map/all_gather | solution.py:45
  257.3 4.0 fusion.21
  261.4 0.0 reduce-scatter.2.cloned.1.call-start
  261.4 155.4 %all-gather.9.cloned.1.call-done = f32[6144,256]{1,0:T(8,128)} async-done(((f32[192,256]{1,0:T(8,128)}), f32[6144,256]{1,0:T(8,128)}) %all-gather.9.cloned.1.call-update) | async-done | bytes 6291472 | tf_op jit(solution)/shard_map/all_gather | solution.py:55
  416.8 3.2 reduce_sum.19
  420.1 1.8 fusion.13
  421.9 111.6 %reduce-scatter.2.cloned.1.call-done = f32[128,256]{1,0:T(8,128)} async-done(((f32[2048,256]{1,0:T(8,128)}), f32[128,256]{1,0:T(8,128)}) %reduce-scatter.2.cloned.1.call-update) | async-done | bytes 131088 | tf_op jit(solution)/shard_map/reduce_scatter | solution.py:57
  533.5 1.6 broadcast_multiply_fusion
  (16 shorter events, 0.2 us)
Async XLA Ops:
  7.2 2.3 copy-start
  7.2 189.1 %all-gather.5.cloned.1.call-start = ((), (), s32[]{:S(2)}) async-start(), calls=%async_computation.1 | async-start | bytes 13369344 | tf_op jit(solution)/shard_map/all_gather | solution.py:48
  9.5 9.6 %copy-start.1 = (bf16[16,4,2048]{2,1,0:T(4,128)(2,1)S(1)}, bf16[16,4,2048]{2,1,0:T(4,128)(2,1)}, u32[]{:S(2)}) copy-start(bf16[16,4,2048]{2,1,0:T(4,128)(2,1)} %param.6) | copy-start | bytes 786436
  39.7 217.6 %all-gather.7.cloned.1.call-start = ((), (), s32[]{:S(2)}) async-start(), calls=%async_computation.2 | async-start | bytes 1671168 | tf_op jit(solution)/shard_map/all_gather | solution.py:45
  40.5 376.3 %all-gather.9.cloned.1.call-start = ((), (), s32[]{:S(2)}) async-start(), calls=%async_computation.4 | async-start | bytes 6488064 | tf_op jit(solution)/shard_map/all_gather | solution.py:55
  40.9 5.7 %collective-permute-start = (f32[192,1,128]{2,1,0:T(1,128)S(1)}, f32[192,1,128]{2,1,0:T(1,128)S(1)}, u32[]{:S(2)}, u32[]{:S(2)}) collective-permute-start(f32[192,1,128]{2,1,0:T(1,128)S(1)} %get-tuple-element.6), channel_id=1, source_target_pairs={{0,16},{16,32},{32,48},{48,64},{64,80},{80,96},{96,112},{112,128},... | collective-permute-start | bytes 294920 | tf_op jit(solution)/shard_map/ppermute | solution.py:18
  45.0 7.5 %collective-permute-start.1 = (f32[192,1,128]{2,1,0:T(1,128)S(1)}, f32[192,1,128]{2,1,0:T(1,128)S(1)}, u32[]{:S(2)}, u32[]{:S(2)}) collective-permute-start(f32[192,1,128]{2,1,0:T(1,128)S(1)} %get-tuple-element.7), channel_id=1, source_target_pairs={{16,0},{32,16},{48,32},{64,48},{80,64},{96,80},{112,96},{128,112},... | collective-permute-start | bytes 294920 | tf_op jit(solution)/shard_map/ppermute | solution.py:19
  53.9 5.4 %collective-permute-start.2 = (f32[192,1,128]{2,1,0:T(1,128)S(1)}, f32[192,1,128]{2,1,0:T(1,128)S(1)}, u32[]{:S(2)}, u32[]{:S(2)}) collective-permute-start(f32[192,1,128]{2,1,0:T(1,128)S(1)} %get-tuple-element.4), channel_id=1, source_target_pairs={{0,16},{16,32},{32,48},{48,64},{64,80},{80,96},{96,112},{112,128},... | collective-permute-start | bytes 294920 | tf_op jit(solution)/shard_map/ppermute | solution.py:18
  57.7 8.8 %collective-permute-start.3 = (f32[192,1,128]{2,1,0:T(1,128)S(1)}, f32[192,1,128]{2,1,0:T(1,128)S(1)}, u32[]{:S(2)}, u32[]{:S(2)}) collective-permute-start(f32[192,1,128]{2,1,0:T(1,128)S(1)} %get-tuple-element.5), channel_id=1, source_target_pairs={{16,0},{32,16},{48,32},{64,48},{80,64},{96,80},{112,96},{128,112},... | collective-permute-start | bytes 294920 | tf_op jit(solution)/shard_map/ppermute | solution.py:19
  261.4 272.2 %reduce-scatter.2.cloned.1.call-start = ((), (), s32[]{:S(2)}) async-start(), calls=%async_computation.3 | async-start | bytes 2228224 | tf_op jit(solution)/shard_map/reduce_scatter | solution.py:57
  416.8 3.2 copy-start.3
  420.1 1.9 copy-start.2
Sparse Core Ops, SparseCore 0:
  39.8 156.4 all-gather.4
  199.5 57.7 all-gather.6
  261.5 155.2 all-gather.8
  422.0 111.4 reduce-scatter.1
